TPU v7x, 512 devices: a whole 4x8x8 slice. The times are simulated.
512 devices in a mesh: grp: 4 (over z_hi), slab: 128 (over y, z_lo, x, core).
Axes of the slice: x: 4, y: 8, z: 8 (z_hi: 4, z_lo: 2; z = z_hi * 2 + z_lo), core: 2. Of those that a mesh axis runs over, the one named last changes fastest.
Arguments:
- points: bfloat16 [128, 4, 3072, 96], P('slab', 'grp'), may hold values from -6 to 6
- slot_mask: int32 [128, 4, 3072], P('slab', 'grp'), may hold values from 0 to 1, as said below
- window_counts: int32 [128, 4], P('slab', 'grp'), may hold values from 24 to 96
- block_gains: float32 [2, 2, 96], replicated, may hold values from 0.25 to 1.75
- qkv_weight: bfloat16 [2, 96, 288], replicated, may hold values from -1 to 1
- out_weight: bfloat16 [2, 96, 96], replicated, may hold values from -0.625 to 0.625
- mlp_in: bfloat16 [2, 96, 384], replicated, may hold values from -0.625 to 0.625
- mlp_out: bfloat16 [2, 384, 96], replicated, may hold values from -0.3125 to 0.3125
- down_weight: bfloat16 [768, 192], replicated, may hold values from -0.21875 to 0.21875
- coarse_gain: float32 [192], replicated, may hold values from 0.25 to 1.75
- coarse_grad: bfloat16 [128, 1536, 192], P('slab'), may hold values from -6 to 6
Outputs:
- coarse: bfloat16 [128, 1536, 192], P('slab')
- fine_grad: bfloat16 [128, 4, 3072, 96], P('slab', 'grp')
- down_grad: float32 [768, 192], replicated
Inputs may be any that keep to these rules, and one draw needn't show every extreme that they name: `slot_mask`: each run of 8 aligned slots holds at least one 1.
All inputs are finite; a program needn't handle non-finite values.
Results may differ from a plain program's by a relative error of at most 0.012.
Values may be sent and summed in bfloat16 or wider, within the bound.
A program may use at most 128 MiB of HBM per device.

v0:
```python
import functools
import math

import jax
import jax.numpy as jnp
from jax import lax
from jax.experimental import pallas as pl
from jax.experimental.pallas import tpu as pltpu
from jax.sharding import PartitionSpec as P

MESH = pl.DeviceIdType.MESH
F32 = jnp.float32
BF = jnp.bfloat16
HEADS = 6
DEPTH = 16
WIDTH = 96
WINDOW = 32
LANES = 128
CHUNK = 512
PARENT = 8
WIDE = 192
EPS = 1e-05
NEG = -1e30
VMEM_LIMIT = 56 * 1024 * 1024


def dot(a, b, ca, cb):
    return lax.dot_general(a, b, (((ca,), (cb,)), ((), ())), preferred_element_type=F32)


def iota(shape, dim):
    return lax.broadcasted_iota(jnp.int32, shape, dim)


def onehot(rows, cols, match):
    return jnp.where(match(iota((rows, cols), 0), iota((rows, cols), 1)), 1.0, 0.0).astype(BF)


def cell_matrix():
    return onehot(LANES, LANES, lambda r, l: r % 16 * PARENT + r // 16 == l)


def norm_rows(value, gain):
    mean = jnp.mean(value, axis=0, keepdims=True)
    centered = value - mean
    spread = jnp.mean(centered * centered, axis=0, keepdims=True)
    return centered * lax.rsqrt(spread + EPS) * gain


def gelu(x):
    return 0.5 * x * (1.0 + lax.erf(x * (0.5**0.5)))


def lane_of(slot):
    return slot % 4 * LANES + slot // WINDOW * 8 + slot % WINDOW // 4


def key_mask(live_row):
    own = iota((WINDOW, LANES), 1) % WINDOW == iota((WINDOW, LANES), 0)
    spread = jnp.where(own, jnp.broadcast_to(live_row, (WINDOW, LANES)), 0.0).astype(BF)
    same = onehot(LANES, LANES, lambda a, b: a // WINDOW == b // WINDOW)
    return (dot(spread, same, 1, 0) > 0.5) | own


def attend(qkv_t, live):
    which = (iota((1, 2 * LANES), 1) % LANES) // WINDOW
    none = jnp.zeros((DEPTH, LANES), BF)
    zero = jnp.zeros((), BF)
    parts = [qkv_t[:, b * LANES : (b + 1) * LANES] for b in range(len(live))]
    keys = [jnp.transpose(p[WIDTH : 2 * WIDTH].astype(F32)).astype(BF) for p in parts]
    masks = [key_mask(row) for row in live]
    scores, spreads = {}, {}
    for b in range(len(live)):
        for pair in range(HEADS // 2):
            cols = []
            for h in (2 * pair, 2 * pair + 1):
                q = parts[b][h * DEPTH : (h + 1) * DEPTH]
                cols.append(jnp.concatenate([q if i == h else none for i in range(HEADS)], 0))
            scores[b, pair] = dot(keys[b], jnp.concatenate(cols, 1), 1, 0)
    for at, score in scores.items():
        s = score.reshape(4, WINDOW, 2 * LANES)
        folded = jnp.where(which == 0, s[0], jnp.where(which == 1, s[1], jnp.where(which == 2, s[2], s[3])))
        mask = masks[at[0]]
        folded = jnp.where(jnp.concatenate([mask, mask], 1), folded, NEG)
        expo = jnp.exp(folded - jnp.max(folded, axis=0, keepdims=True))
        scale = 1.0 / jnp.sum(expo, axis=0, keepdims=True)
        half = expo.astype(BF)
        spreads[at] = jnp.concatenate([jnp.where(which == w, half, zero) for w in range(4)], 0), scale
    outs = []
    for b in range(len(live)):
        rows = []
        for pair in range(HEADS // 2):
            spread, scale = spreads[b, pair]
            first = 2 * WIDTH + pair * 2 * DEPTH
            mixed = dot(parts[b][first : first + 2 * DEPTH], spread, 1, 0) * scale
            rows += [mixed[:DEPTH, :LANES], mixed[DEPTH:, LANES:]]
        outs.append(jnp.concatenate(rows, 0).astype(BF))
    return jnp.concatenate(outs, 1)


def project(w_t, normed):
    qkv = dot(w_t, normed, 1, 0)
    return jnp.concatenate([qkv[:WIDTH] * (DEPTH**-0.5), qkv[WIDTH:]], 0).astype(BF)


def feed_forward(state, gain, w_in_t, w_back_t):
    inner = norm_rows(state, gain).astype(BF)
    parts = [dot(w_in_t, inner[:, at : at + 256], 1, 0) for at in range(0, state.shape[1], 256)]
    backs = [dot(w_back_t, gelu(p).astype(BF), 1, 0) for p in parts]
    return state + jnp.concatenate(backs, 1)


def turn(w):
    return jnp.transpose(w.astype(F32)).astype(BF)


def axis_ids():
    slab, grp = lax.axis_index("slab"), lax.axis_index("grp")
    core, x, z_lo, y = slab % 2, (slab // 2) % 4, (slab // 8) % 2, slab // 16
    return core, x, y, grp * 2 + z_lo


def device_at(core, x, y, z):
    return {"slab": ((y * 2 + z % 2) * 4 + x) * 2 + core, "grp": z // 2}


def send(src, dst, send_sem, recv_sem, peer):
    return pltpu.make_async_remote_copy(
        src_ref=src, dst_ref=dst, send_sem=send_sem, recv_sem=recv_sem, device_id=peer, device_id_type=MESH
    )


def whole_kernel(
    points_ref, mask_ref, count_ref, gains_ref, qkv_ref, out_ref, in_ref, back_ref, weight_ref, gain_ref, cot_ref,
    run_ref, fine_ref, grad_ref,
    wq, wo, wi, gains, gain, swap, wide, states, lives, lived, dealt, there, got, answer, heard, pooled, cot, loaded, term,
    crossed, summed, lines, mine, planes, pieces, column, whole,
    cot_sem, load_sem, live_sems, there_sems, answer_sems, run_sems, sems,
):
    core, x, y, z = axis_ids()
    me = lax.axis_index("grp")
    slab = lax.axis_index("slab")
    chunks, cells = there.shape[0], pooled.shape[0]
    group = [{"slab": slab, "grp": (me + d) % 4} for d in (1, 2, 3)]
    across = device_at(1 - core, x, y, z)
    beside = [device_at(core, (x + d) % 4, y, z) for d in range(1, 4)]
    along = [device_at(core, x, (y + d) % 8, z) for d in range(1, 8)]
    above = [device_at(core, x, y, (z + d) % 8) for d in range(1, 8)]
    barrier = pltpu.get_barrier_semaphore()
    diagonal = [device_at(1 - core, (x + d) % 4, y, z) for d in range(1, 4)]
    peers = [across] + beside + diagonal + along + above
    for peer in peers:
        pl.semaphore_signal(barrier, inc=1, device_id=peer, device_id_type=MESH)

    fetch = pltpu.make_async_copy(cot_ref.at[:, pl.ds(pl.multiple_of(me * cells, LANES), cells)], cot, cot_sem)
    fetch.start()

    load = pltpu.make_async_copy(weight_ref, loaded, load_sem)
    load.start()

    wq[0] = turn(qkv_ref[0])
    wo[0] = turn(out_ref[0])
    wi[0] = turn(in_ref[0])
    gains[...] = jnp.transpose(jnp.concatenate([gains_ref[...], gains_ref[...]], 0))
    gain[...] = jnp.transpose(jnp.broadcast_to(gain_ref[...], (8, WIDE)))
    swap[0] = onehot(CHUNK, CHUNK, lambda a, b: lane_of(a) == b)
    swap[1] = onehot(CHUNK, CHUNK, lambda a, b: lane_of(b) == a)
    blocks = mask_ref.shape[0]
    window = iota((blocks, LANES), 0) * 4 + iota((blocks, LANES), 1) // WINDOW
    live = jnp.where(window < count_ref[...], mask_ref[...].astype(F32), 0.0)
    lived[me] = live
    for i in range(chunks):
        lives[i] = live[i * 4 : (i + 1) * 4]

    def live_copies():
        return [
            send(lived.at[me], lived.at[me], live_sems.at[0, d - 1], live_sems.at[1, d - 1], group[d - 1])
            for d in (2, 1, 3)
        ]

    def copies(i, src, dst, table):
        return [
            send(src.at[i, (me + d) % 4], dst.at[i, me], table.at[0, i, d - 1], table.at[1, i, d - 1], group[d - 1])
            for d in (2, 1, 3)
        ]

    def part(i, src, dst, table, rows):
        rows = dot(rows, swap[0], 1, 0).astype(BF)
        for r in range(4):
            src[i, r] = rows[:, r * LANES : (r + 1) * LANES]
        dst[i, me] = src[i, me]
        for copy in copies(i, src, dst, table):
            copy.start()

    def join(i, src, dst, table):
        for copy in copies(i, src, dst, table):
            copy.wait_recv()
        return dot(jnp.concatenate([dst[i, g] for g in range(4)], 1), swap[1], 1, 0).astype(BF)

    def rows_of(table, at):
        return [table[i][b : b + 1] for i in at for b in range(4)]

    @pl.loop(0, chunks // 2)
    def _(i):
        state = points_ref[:, pl.ds(pl.multiple_of(i * 2 * CHUNK, CHUNK), 2 * CHUNK)].astype(F32)
        qkv = project(wq[0], norm_rows(state, gains[:, 0:1]).astype(BF))
        state = state + dot(wo[0], attend(qkv, rows_of(lives, (2 * i, 2 * i + 1))), 1, 0)
        state = feed_forward(state, gains[:, 1:2], wi[0], back_ref[0])
        states[2 * i] = state[:, :CHUNK]
        states[2 * i + 1] = state[:, CHUNK:]
        normed = norm_rows(state, gains[:, 2:3]).astype(BF)

        @pl.when(i == 0)
        def _():
            pl.semaphore_wait(barrier, len(peers))
            for copy in live_copies():
                copy.start()

        part(2 * i, there, got, there_sems, normed[:, :CHUNK])
        part(2 * i + 1, there, got, there_sems, normed[:, CHUNK:])

    wq[1] = turn(qkv_ref[1])
    wo[1] = turn(out_ref[1])
    wi[1] = turn(in_ref[1])
    load.wait()
    for c in range(PARENT):
        wide[:, c * LANES : (c + 1) * LANES] = jnp.concatenate(
            [loaded[:, c * WIDTH : (c + 1) * WIDTH], jnp.zeros((WIDE, LANES - WIDTH), BF)], 1
        )
    for copy in live_copies():
        copy.wait()
    total = jnp.zeros((blocks, LANES), F32)
    for g in range(4):
        pick = onehot(
            LANES,
            LANES,
            lambda a, b: (b % 4 == g) & (a == b - g + me),
        )
        total = total + dot(lived[g].astype(BF), pick, 1, 0)
    for i in range(chunks):
        dealt[i] = total[i * 4 : (i + 1) * 4]

    @pl.loop(0, chunks)
    def _(i):
        qkv = project(wq[1], join(i, there, got, there_sems))
        part(i, answer, heard, answer_sems, attend(qkv, rows_of(dealt, (i,))))

    @pl.loop(0, chunks)
    def _(i):
        state = states[i] + dot(wo[1], join(i, answer, heard, answer_sems), 1, 0)
        state = feed_forward(state, gains[:, 3:4], wi[1], back_ref[1])
        deal = cell_matrix()
        row = rows_of(lives, (i,))
        for b in range(4):
            fine = state[:, b * LANES : (b + 1) * LANES].astype(BF).astype(F32) * row[b]
            fine = jnp.concatenate([fine.astype(BF), jnp.zeros((LANES - WIDTH, LANES), BF)], 0)
            cell = dot(deal, fine, 1, 1).astype(BF)
            at = pl.ds(pl.multiple_of(i * (CHUNK // PARENT) + b * 16, 16), 16)
            for c in range(PARENT):
                pooled[at, c * LANES : (c + 1) * LANES] = cell[c * 16 : (c + 1) * 16]

    fetch.wait()
    every = pooled[...]
    weight = wide[...]
    column_gain = gain[:, 0:1]
    pre = dot(weight, every, 1, 1)
    centered = pre - jnp.mean(pre, axis=0, keepdims=True)
    scale = lax.rsqrt(jnp.mean(centered * centered, axis=0, keepdims=True) + EPS)
    unit = centered * scale
    slope = cot[...].astype(F32) * column_gain
    slope = slope - jnp.mean(slope, axis=0, keepdims=True) - unit * jnp.mean(slope * unit, axis=0, keepdims=True)
    half = (slope * scale).astype(BF)
    order = [(1 - core) * 4, core * 4]
    for c in range(PARENT):
        term[c] = dot(half, every[:, c * LANES : (c + 1) * LANES], 1, 0).astype(BF)
    first = send(term.at[pl.ds(order[0], 4)], crossed, sems.at[0, 0], sems.at[1, 0], across)
    first.start()

    ours = pl.ds(pl.multiple_of(me * cells, LANES), cells)
    run_ref[:, ours] = (unit * column_gain).astype(BF)
    shares = []

    def share(pieces_now):
        for piece in pieces_now:
            lanes = pl.ds(pl.multiple_of(me * cells + piece // 2 * LANES, LANES), LANES)
            spot = run_ref.at[piece % 2 * WIDTH : piece % 2 * WIDTH + WIDTH, lanes]
            for d in (2, 1, 3):
                shares.append(
                    send(spot, spot, run_sems.at[0, piece, d - 1], run_sems.at[1, piece, d - 1], group[d - 1])
                )
                shares[-1].start()

    sent = [first]
    first.wait_recv()
    for i in range(4):
        summed[i] = (term[order[1] + i].astype(F32) + crossed[i].astype(F32)).astype(BF)
    moves = []
    for d in (2, 1, 3):
        moves.append(send(summed.at[(x + d) % 4], lines.at[d - 1], sems.at[0, d], sems.at[1, d], beside[d - 1]))
        moves[-1].start()
    share((0,))

    back = dot(half, weight, 0, 0).astype(BF)
    deal = cell_matrix()
    for b in range(blocks):
        cell = jnp.concatenate(
            [back[b * 16 : (b + 1) * 16, c * LANES : (c + 1) * LANES] for c in range(PARENT)], 0
        )
        fine = dot(cell, deal, 0, 0)[:WIDTH] * lives[b // 4, b % 4 : b % 4 + 1]
        fine_ref[:, b * LANES : (b + 1) * LANES] = fine.astype(BF)

    for move in moves:
        move.wait_recv()
    sent += moves
    total = summed[x].astype(F32)
    for d in range(3):
        total = total + lines[d].astype(F32)
    mine[:WIDE] = total.astype(BF)
    mine[WIDE:] = jnp.zeros((256 - WIDE, LANES), BF)
    moves = []
    for d in (4, 3, 5, 2, 6, 1, 7):
        to = pl.ds(pl.multiple_of((y + d) % 8 * 32, 32), 32)
        moves.append(send(mine.at[to], planes.at[d - 1], sems.at[0, 3 + d], sems.at[1, 3 + d], along[d - 1]))
        moves[-1].start()
    share((1, 2))
    for move in moves:
        move.wait_recv()
    sent += moves
    row = pl.ds(pl.multiple_of(y * 32, 32), 32)
    total = mine[row].astype(F32)
    for d in range(7):
        total = total + planes[d].astype(F32)
    pieces[z] = total.astype(BF)
    moves = []
    for d in (4, 3, 5, 2, 6, 1, 7):
        moves.append(send(pieces.at[z], pieces.at[z], sems.at[0, 10 + d], sems.at[1, 10 + d], above[d - 1]))
        moves[-1].start()
    share((3,))
    for move in moves:
        move.wait_recv()
    sent += moves
    total = pieces[0].astype(F32)
    for i in range(1, 8):
        total = total + pieces[i].astype(F32)
    column[row] = total.astype(BF)
    moves = []
    for d in (4, 3, 5, 2, 6, 1, 7):
        moves.append(send(column.at[row], column.at[row], sems.at[0, 17 + d], sems.at[1, 17 + d], along[d - 1]))
        moves[-1].start()
    share((4, 5))
    for move in moves:
        move.wait_recv()
    sent += moves
    spot = core * 4 + x
    whole[spot] = column[:WIDE]
    moves = []
    for d in (2, 1, 3):
        for other in range(2):
            at = 24 + d * 2 + other
            peer = device_at((core + other) % 2, (x + d) % 4, y, z)
            moves.append(send(whole.at[spot], whole.at[spot], sems.at[0, at], sems.at[1, at], peer))
            moves[-1].start()
    moves.append(send(whole.at[spot], whole.at[spot], sems.at[0, 25], sems.at[1, 25], across))
    moves[-1].start()
    for move in moves:
        move.wait_recv()
    sent += moves
    for c in range(PARENT):
        grad_ref[:, c * WIDTH : (c + 1) * WIDTH] = whole[c][:, :WIDTH].astype(F32) * (
            1.0 / math.sqrt(lax.axis_size("slab") * run_ref.shape[1])
        )
    for copy in shares:
        copy.wait()
    for copy in sent:
        copy.wait_send()

    @pl.loop(0, chunks)
    def _(i):
        for copy in copies(i, there, got, there_sems) + copies(i, answer, heard, answer_sems):
            copy.wait_send()


def leave_kernel(run_ref, fine_ref, grad_ref, run_out, fine_out, grad_out, sems):
    pairs = ((run_ref, run_out), (fine_ref, fine_out), (grad_ref, grad_out))
    moves = [pltpu.make_async_copy(a, b, sems.at[i]) for i, (a, b) in enumerate(pairs)]
    for move in moves:
        move.start()
    for move in moves:
        move.wait()


def local(points, slot_mask, window_counts, block_gains, qkv_weight, out_weight, mlp_in, mlp_out, down_weight,
          coarse_gain, coarse_grad):
    rows = points.shape[2]
    blocks, cells, chunks = rows // LANES, rows // PARENT, rows // CHUNK
    vmem = pl.BlockSpec(memory_space=pltpu.VMEM)
    sems = pltpu.SemaphoreType.DMA
    run, fine, grad = pl.pallas_call(
        whole_kernel,
        in_specs=[vmem] * 8 + [pl.BlockSpec(memory_space=pl.ANY), vmem, pl.BlockSpec(memory_space=pl.ANY)],
        out_specs=[vmem] * 3,
        out_shape=[
            pltpu.VMEM((WIDE, 4 * cells), BF),
            pltpu.VMEM((WIDTH, rows), BF),
            pltpu.VMEM((WIDE, PARENT * WIDTH), F32),
        ],
        scratch_shapes=[
            pltpu.VMEM((2, 3 * WIDTH, WIDTH), BF),
            pltpu.VMEM((2, WIDTH, WIDTH), BF),
            pltpu.VMEM((2, 4 * WIDTH, WIDTH), BF),
            pltpu.VMEM((WIDTH, 8), F32),
            pltpu.VMEM((WIDE, 8), F32),
            pltpu.VMEM((2, CHUNK, CHUNK), BF),
            pltpu.VMEM((WIDE, PARENT * LANES), BF),
            pltpu.VMEM((chunks, WIDTH, CHUNK), F32),
            pltpu.VMEM((chunks, 4, LANES), F32),
            pltpu.VMEM((4, blocks, LANES), F32),
            pltpu.VMEM((chunks, 4, LANES), F32),
            pltpu.VMEM((chunks, 4, WIDTH, LANES), BF),
            pltpu.VMEM((chunks, 4, WIDTH, LANES), BF),
            pltpu.VMEM((chunks, 4, WIDTH, LANES), BF),
            pltpu.VMEM((chunks, 4, WIDTH, LANES), BF),
            pltpu.VMEM((cells, PARENT * LANES), BF),
            pltpu.VMEM((WIDE, cells), BF),
            pltpu.VMEM((WIDE, PARENT * WIDTH), BF),
            pltpu.VMEM((PARENT, WIDE, LANES), BF),
            pltpu.VMEM((4, WIDE, LANES), BF),
            pltpu.VMEM((4, WIDE, LANES), BF),
            pltpu.VMEM((3, WIDE, LANES), BF),
            pltpu.VMEM((256, LANES), BF),
            pltpu.VMEM((7, 32, LANES), BF),
            pltpu.VMEM((8, 32, LANES), BF),
            pltpu.VMEM((256, LANES), BF),
            pltpu.VMEM((8, WIDE, LANES), BF),
            sems,
            sems,
            sems((2, 3)),
            sems((2, chunks, 3)),
            sems((2, chunks, 3)),
            sems((2, 6, 3)),
            sems((2, 32)),
        ],
        compiler_params=pltpu.CompilerParams(
            collective_id=1, has_side_effects=True, vmem_limit_bytes=VMEM_LIMIT
        ),
    )(
        points.reshape(rows, WIDTH).T, slot_mask.reshape(blocks, LANES), window_counts, block_gains.reshape(4, WIDTH),
        qkv_weight, out_weight, mlp_in, jnp.swapaxes(mlp_out, 1, 2), down_weight.T, coarse_gain.reshape(1, WIDE),
        coarse_grad.reshape(4 * cells, WIDE).T,
    )
    run, fine, grad = pl.pallas_call(
        leave_kernel,
        in_specs=[vmem] * 3,
        out_specs=[pl.BlockSpec(memory_space=pl.ANY)] * 3,
        out_shape=[jax.ShapeDtypeStruct(v.shape, v.dtype) for v in (run, fine, grad)],
        scratch_shapes=[sems((3,))],
        compiler_params=pltpu.CompilerParams(vmem_limit_bytes=VMEM_LIMIT),
    )(*[pltpu.with_memory_space_constraint(v, pltpu.VMEM) for v in (run, fine, grad)])
    return run.T.reshape(1, 4 * cells, WIDE), fine.T.reshape(1, 1, rows, WIDTH), grad.T


def solution(mesh):
    placed = (
        P("slab", "grp", None, None), P("slab", "grp", None), P("slab", "grp"), P(), P(), P(), P(), P(), P(), P(),
        P("slab", None, None),
    )
    return jax.shard_map(
        local,
        mesh=mesh,
        in_specs=placed,
        out_specs=(P("slab", None, None), P("slab", "grp", None, None), P()),
        check_vma=False,
    )
```

profile of v0, /device:TPU:1, one launch (start us, length us, event | category | flops | bytes accessed | tf_op | source)
XLA Modules:
  0.0 81.7 jit_solution(10703178896734869626)
XLA Ops:
  1.3 79.2 %shard_map.130 = (bf16[192,1536]{1,0:T(8,128)(2,1)S(1)}, bf16[96,3072]{1,0:T(8,128)(2,1)S(1)}, f32[192,768]{1,0:T(8,128)S(1)}) custom-call(bf16[96,3072]{1,0:T(8,128)(2,1)} %bitcast.18, s32[24,128]{1,0:T(8,128)} %bitcast.22, s32[1,1]{1,0:T(1,128)S(6)} %copy.14.count_ref, f32[4,96]{1,0:T(4,128)} %bitcast.23, bf16[2,96,288]{2,1,0:T(8,128)(2,1)} %qkv_ref.1, ...), custom_call_target="tpu_custom_call" | custom-call | tf_op jit(solution)/shard_map/pallas_call | solution.py:398
  80.5 1.2 %shard_map.131 = (bf16[192,1536]{1,0:T(8,128)(2,1)}, bf16[96,3072]{1,0:T(8,128)(2,1)}, f32[192,768]{1,0:T(8,128)}) custom-call(bf16[192,1536]{1,0:T(8,128)(2,1)S(1)} %get-tuple-element.9.run_ref, bf16[96,3072]{1,0:T(8,128)(2,1)S(1)} %get-tuple-element.10.fine_ref, f32[192,768]{1,0:T(8,128)S(1)} %get-tuple-element.11.grad_ref), custom_call_target="tpu_custom_call" | custom-call | tf_op jit(solution)/shard_map/pallas_call | solution.py:451
where the time goes:
time: 81.8 us; the launch traced here: 81.7 us
  Pallas kernels  80.4 us (98%)
  between operations  1.29 us (2%)
    pallas_call x1, Pallas kernels, local(): pl.pallas_call(whole_kernel, in_specs=[vmem] * 8 + [pl.BlockSpec(memory_s...  79.2 us

commit v1 on v0

--- a/solution.py
+++ b/solution.py
@@ -200,14 +200,13 @@
     def rows_of(table, at):
         return [table[i][b : b + 1] for i in at for b in range(4)]
 
-    @pl.loop(0, chunks // 2)
+    @pl.loop(0, chunks)
     def _(i):
-        state = points_ref[:, pl.ds(pl.multiple_of(i * 2 * CHUNK, CHUNK), 2 * CHUNK)].astype(F32)
+        state = points_ref[:, pl.ds(pl.multiple_of(i * CHUNK, CHUNK), CHUNK)].astype(F32)
         qkv = project(wq[0], norm_rows(state, gains[:, 0:1]).astype(BF))
-        state = state + dot(wo[0], attend(qkv, rows_of(lives, (2 * i, 2 * i + 1))), 1, 0)
+        state = state + dot(wo[0], attend(qkv, rows_of(lives, (i,))), 1, 0)
         state = feed_forward(state, gains[:, 1:2], wi[0], back_ref[0])
-        states[2 * i] = state[:, :CHUNK]
-        states[2 * i + 1] = state[:, CHUNK:]
+        states[i] = state
         normed = norm_rows(state, gains[:, 2:3]).astype(BF)
 
         @pl.when(i == 0)
@@ -216,8 +215,7 @@
             for copy in live_copies():
                 copy.start()
 
-        part(2 * i, there, got, there_sems, normed[:, :CHUNK])
-        part(2 * i + 1, there, got, there_sems, normed[:, CHUNK:])
+        part(i, there, got, there_sems, normed)
 
     wq[1] = turn(qkv_ref[1])
     wo[1] = turn(out_ref[1])
@@ -310,8 +308,7 @@
         fine_ref[:, b * LANES : (b + 1) * LANES] = fine.astype(BF)
 
     for move in moves:
-        move.wait_recv()
-    sent += moves
+        move.wait()
     total = summed[x].astype(F32)
     for d in range(3):
         total = total + lines[d].astype(F32)
@@ -324,8 +321,7 @@
         moves[-1].start()
     share((1, 2))
     for move in moves:
-        move.wait_recv()
-    sent += moves
+        move.wait()
     row = pl.ds(pl.multiple_of(y * 32, 32), 32)
     total = mine[row].astype(F32)
     for d in range(7):
@@ -337,8 +333,7 @@
         moves[-1].start()
     share((3,))
     for move in moves:
-        move.wait_recv()
-    sent += moves
+        move.wait()
     total = pieces[0].astype(F32)
     for i in range(1, 8):
         total = total + pieces[i].astype(F32)
@@ -349,8 +344,7 @@
         moves[-1].start()
     share((4, 5))
     for move in moves:
-        move.wait_recv()
-    sent += moves
+        move.wait()
     spot = core * 4 + x
     whole[spot] = column[:WIDE]
     moves = []
@@ -363,8 +357,7 @@
     moves.append(send(whole.at[spot], whole.at[spot], sems.at[0, 25], sems.at[1, 25], across))
     moves[-1].start()
     for move in moves:
-        move.wait_recv()
-    sent += moves
+        move.wait()
     for c in range(PARENT):
         grad_ref[:, c * WIDTH : (c + 1) * WIDTH] = whole[c][:, :WIDTH].astype(F32) * (
             1.0 / math.sqrt(lax.axis_size("slab") * run_ref.shape[1])

time: 81.8 us -> 77.6 us (0.949)
  Pallas kernels: 80.4 us -> 76.1 us
    pallas_call x1, Pallas kernels: 79.2 us -> 74.9 us  [local(): pl.pallas_call(whole_kernel, in_specs=[vmem] * 8 + [pl.BlockSpec(memory_s...]
where the time goes in v1:
time: 77.6 us; the launch traced here: 77.4 us
  Pallas kernels  76.1 us (98%)
  between operations  1.29 us (2%)
    pallas_call x1, Pallas kernels, local(): pl.pallas_call(whole_kernel, in_specs=[vmem] * 8 + [pl.BlockSpec(memory_s...  74.9 us

profile of v1, /device:TPU:1, one launch (start us, length us, event | category | flops | bytes accessed | tf_op | source)
XLA Modules:
  0.0 77.4 jit_solution(5441384692812059815)
XLA Ops:
  1.3 74.9 %shard_map.130 = (bf16[192,1536]{1,0:T(8,128)(2,1)S(1)}, bf16[96,3072]{1,0:T(8,128)(2,1)S(1)}, f32[192,768]{1,0:T(8,128)S(1)}) custom-call(bf16[96,3072]{1,0:T(8,128)(2,1)} %bitcast.18, s32[24,128]{1,0:T(8,128)} %bitcast.22, s32[1,1]{1,0:T(1,128)S(6)} %copy.14.count_ref, f32[4,96]{1,0:T(4,128)} %bitcast.23, bf16[2,96,288]{2,1,0:T(8,128)(2,1)} %qkv_ref.1, ...), custom_call_target="tpu_custom_call" | custom-call | tf_op jit(solution)/shard_map/pallas_call | solution.py:391
  76.2 1.2 %shard_map.131 = (bf16[192,1536]{1,0:T(8,128)(2,1)}, bf16[96,3072]{1,0:T(8,128)(2,1)}, f32[192,768]{1,0:T(8,128)}) custom-call(bf16[192,1536]{1,0:T(8,128)(2,1)S(1)} %get-tuple-element.9.run_ref, bf16[96,3072]{1,0:T(8,128)(2,1)S(1)} %get-tuple-element.10.fine_ref, f32[192,768]{1,0:T(8,128)S(1)} %get-tuple-element.11.grad_ref), custom_call_target="tpu_custom_call" | custom-call | tf_op jit(solution)/shard_map/pallas_call | solution.py:444
